TPU v7x, 32 devices: a whole 2x2x4 slice. The times are simulated.
32 devices in a mesh: group: 2 (over x), dx: 16 (over z, y, core).
Axes of the slice: x: 2, y: 2, z: 4, core: 2. Of those that a mesh axis runs over, the one named last changes fastest.
Arguments:
- points: bfloat16 [16384, 1024], P(('group', 'dx')), parts along dimension 0, may hold values from -6 to 6
- cotangent: bfloat16 [16384, 1024], P(('group', 'dx')), parts along dimension 0, may hold values from -96 to 96
- counts: int32 [32], P(('group', 'dx')), parts along dimension 0, may hold values from 170 to 512, as said below
- w_query: bfloat16 [1024, 1024], replicated, may hold values from -0.1875 to 0.1875
- w_key: bfloat16 [1024, 1024], replicated, may hold values from -0.1875 to 0.1875
- w_value: bfloat16 [1024, 1024], replicated, may hold values from -0.1875 to 0.1875
- gain_key: float32 [1024], replicated, may hold values from 0.25 to 1.75
- bias_key: float32 [1024], replicated, may hold values from -3 to 3
- gain_value: float32 [1024], replicated, may hold values from 0.25 to 1.75
- bias_value: float32 [1024], replicated, may hold values from -3 to 3
Outputs:
- grad_points: bfloat16 [16384, 1024], P(('group', 'dx')), parts along dimension 0
There are 2 independent parts, one for each index of `group`. A program takes and returns all parts, laid end to end along the dimension named above; an argument that names none is the same for every part. Nothing has to cross between parts.
Inputs may be any that keep to these rules, and one draw needn't show every extreme that they name: `counts`: live points of each tile; some tile of every slab holds 512.
All inputs are finite; a program needn't handle non-finite values.
Results may differ from a plain program's by a relative error of at most 0.006.
Values sent between devices are 32-bit elements; how exact they have to be, the bound alone decides.
A program may use at most 64 MiB of HBM per device.

v0:
```python
import jax
import jax.numpy as jnp
from jax import lax
from jax.sharding import PartitionSpec as P

HEADS = 8
eps = 1e-05


def head_norm(raw, heads):
    grouped = raw.reshape(raw.shape[0], heads, -1)
    center = grouped - jnp.mean(grouped, axis=2, keepdims=True)
    inverse = lax.rsqrt(jnp.mean(center * center, axis=2, keepdims=True) + eps)
    return (center * inverse, inverse)


def norm_back(grad, gain, normed, inverse, heads):
    scaled = grad * gain.reshape(heads, -1)
    inner = scaled - jnp.mean(scaled, axis=2, keepdims=True)
    inner = inner - normed * jnp.mean(scaled * normed, axis=2, keepdims=True)
    return (inverse * inner).reshape(grad.shape[0], -1).astype(jnp.bfloat16)


def body(
    points, cotangent, counts, w_query, w_key, w_value, gain_key, bias_key, gain_value, bias_value
):
    rows = points.shape[0]
    heads = HEADS
    live = (lax.iota(jnp.int32, rows) < counts[0]).astype(jnp.float32)[:, None]
    live_h = live[:, :, None]
    own_count = counts[0].astype(jnp.float32)
    total = lax.psum(own_count, "dx")
    key_hat, key_inv = head_norm(jnp.dot(points, w_key, preferred_element_type=jnp.float32), heads)
    value_hat, value_inv = head_norm(
        jnp.dot(points, w_value, preferred_element_type=jnp.float32), heads
    )
    keys = (live_h * (key_hat * gain_key.reshape(heads, -1) + bias_key.reshape(heads, -1))).astype(
        jnp.bfloat16
    )
    values = (
        live_h * (value_hat * gain_value.reshape(heads, -1) + bias_value.reshape(heads, -1))
    ).astype(jnp.bfloat16)
    kv_local = jnp.einsum("nhi,nhj->hij", keys, values, preferred_element_type=jnp.float32)
    cot = cotangent.reshape(rows, heads, -1)
    kv_sum = lax.psum(kv_local, "dx")
    query = jnp.dot(points, w_query, preferred_element_type=jnp.float32).astype(jnp.bfloat16)
    masked_query = (query * live.astype(jnp.bfloat16)).reshape(rows, heads, -1)
    qdy_local = jnp.einsum("nhi,nhj->hij", masked_query, cot, preferred_element_type=jnp.float32)
    qdy_sum = lax.psum(qdy_local, "dx")
    gram = (kv_sum / total).astype(jnp.bfloat16)
    dgram = (qdy_sum / total).astype(jnp.bfloat16)
    dquery = (
        (live_h * jnp.einsum("nhj,hij->nhi", cot, gram, preferred_element_type=jnp.float32))
        .reshape(rows, -1)
        .astype(jnp.bfloat16)
    )
    dkeys = jnp.einsum("nhj,hij->nhi", values, dgram, preferred_element_type=jnp.float32)
    dvalues = jnp.einsum("nhi,hij->nhj", keys, dgram, preferred_element_type=jnp.float32)
    dkey_raw = norm_back(dkeys, gain_key, key_hat, key_inv, heads)
    dvalue_raw = norm_back(dvalues, gain_value, value_hat, value_inv, heads)
    grad = jnp.dot(dquery, w_query.T, preferred_element_type=jnp.float32)
    grad = grad + jnp.dot(dkey_raw, w_key.T, preferred_element_type=jnp.float32)
    grad = grad + jnp.dot(dvalue_raw, w_value.T, preferred_element_type=jnp.float32)
    return grad.astype(jnp.bfloat16)


def solution(mesh):
    placed = (
        P(("group", "dx"), None),
        P(("group", "dx"), None),
        P(("group", "dx")),
        P(),
        P(),
        P(),
        P(),
        P(),
        P(),
        P(),
    )
    return jax.shard_map(
        body, mesh=mesh, in_specs=placed, out_specs=P(("group", "dx"), None), check_vma=False
    )
```

profile of v0, /device:TPU:0, one launch (start us, length us, event | category | flops | bytes accessed | tf_op | source)
XLA Modules:
  0.0 156.2 jit_solution(9435731812244880489)
XLA Ops:
  6.5 0.0 copy-start
  6.5 0.0 all-reduce.3.cloned.1.call-start
  6.5 3.3 %convolution_bitcast_fusion = f32[64,8,8,128]{3,1,2,0:T(8,128)S(1)} fusion(bf16[512,1024]{1,0:T(8,128)(2,1)} %param.10, bf16[1024,1024]{1,0:T(8,128)(2,1)} %param.15), kind=kOutput, calls=%fused_computation.22 | convolution fusion | flops 1073741824 | bytes 5242880 | tf_op jit(solution)/shard_map/dot_general | solution.py:35
  9.8 1.8 %copy.72 = f32[64,8,8,128]{3,2,1,0:T(8,128)} copy(f32[64,8,8,128]{3,1,2,0:T(8,128)S(1)} %convolution_bitcast_fusion) | data formatting | bytes 4194304
  11.6 3.0 %copy.57 = f32[512,8,128]{0,2,1:T(8,128)} copy(f32[512,8,128]{2,1,0:T(8,128)} %bitcast.70) | data formatting | bytes 4194304 | tf_op jit(solution)/shard_map/reshape | solution.py:11
  14.6 0.0 copy-start.11
  14.6 2.3 %reduce_sum.74 = f32[512,8]{1,0:T(8,128)S(1)} reduce(f32[512,8,128]{2,1,0:T(8,128)} %bitcast.71, f32[]{:T(128)} %constant.11.clone.1), dimensions={2}, to_apply=%region_2.0 | reduce | flops 520192 | bytes 2113540 | tf_op jit(solution)/shard_map/reduce_sum | solution.py:12
  16.9 0.0 copy-done
  16.9 0.0 copy-done.11
  16.9 1.3 convolution_bitcast_fusion.1
  18.2 1.8 %copy.71 = f32[64,8,8,128]{3,2,1,0:T(8,128)} copy(f32[64,8,8,128]{3,1,2,0:T(8,128)S(1)} %convolution_bitcast_fusion.1) | data formatting | bytes 4194304
  20.0 2.9 %copy.55 = f32[512,8,128]{0,2,1:T(8,128)} copy(f32[512,8,128]{2,1,0:T(8,128)} %bitcast.68) | data formatting | bytes 4194304 | tf_op jit(solution)/shard_map/reshape | solution.py:11
  22.9 2.2 %reduce_sum.72 = f32[512,8]{1,0:T(8,128)S(1)} reduce(f32[512,8,128]{2,1,0:T(8,128)} %bitcast.69, f32[]{:T(128)} %constant.11.clone.1), dimensions={2}, to_apply=%region_0.0 | reduce | flops 520192 | bytes 2113540 | tf_op jit(solution)/shard_map/reduce_sum | solution.py:12
  25.1 0.1 copy.56
  25.2 0.1 copy.54
  26.0 4.1 %fusion.8 = bf16[512,1024]{1,0:T(8,128)(2,1)} fusion(bf16[512,1024]{1,0:T(8,128)(2,1)} %param.10, bf16[1024,1024]{1,0:T(8,128)(2,1)} %param.13, bf16[512]{0:T(512)(128)(2,1)S(1)} %get-tuple-element.14), kind=kOutput, calls=%fused_computation.25 | convolution fusion | flops 1074790400 | bytes 4195328 | tf_op jit(solution)/shard_map/dot_general | solution.py:46
  30.2 1.5 copy.69
  31.7 0.0 copy-start.3
  31.7 0.0 copy-start.5
  31.7 2.0 %multiply_reduce_fusion = f32[512,8]{0,1:T(8,128)S(1)} fusion(f32[512,8,128]{0,2,1:T(8,128)} %copy.57, f32[512,8]{0,1:T(8,128)S(1)} %broadcast_multiply_fusion.4), kind=kLoop, calls=%fused_computation.17 | loop fusion | flops 1568768 | bytes 2129920 | tf_op jit(solution)/shard_map/reduce_sum | solution.py:13
  33.7 0.2 copy-done.3
  33.9 0.0 copy-start.1
  33.9 0.0 copy-start.7
  33.9 0.0 copy-start.8
  33.9 0.0 copy-start.14
  33.9 0.0 copy-start.15
  33.9 0.3 multiply_reduce_fusion.1
  34.2 0.0 copy-done.5
  34.2 1.3 fusion.9
  35.5 0.0 copy-done.1
  35.5 0.0 copy-done.7
  35.5 0.0 copy-done.8
  35.6 0.0 copy-done.14
  35.6 0.0 copy-done.15
  35.6 2.0 %fusion.18 = f32[8,128,128]{2,1,0:T(8,128)} fusion(f32[512,8,128]{0,2,1:T(8,128)S(1)} %copy-done.3, f32[8,128]{1,0:T(8,128)S(1)} %bitcast.83, f32[8,128]{1,0:T(8,128)S(1)} %bitcast.75, f32[512,8]{0,1:T(8,128)S(1)} %get-tuple-element.16, f32[512,8]{0,1:T(8,128)S(1)} %broadcast_multiply_fusion.5, f32[512]{0:T(512)S(1)} %get-tuple-element.13, ...), kind=kOutput, calls=%fused_computation.46 | convolution fusion | flops 140509184 | bytes 4802560 | tf_op jit(solution)/shard_map/nhi,nhj->hij/dot_general | solution.py:43
  37.5 0.0 all-reduce.3.cloned.1.call-update
  37.6 35.9 %psum.22 = f32[]{:T(128)} all-reduce(f32[]{:T(128)S(6)} %convert_element_type.64), channel_id=1, replica_groups=mesh['group'=2,'dx'=16] {'dx'}, use_global_device_ids=true, to_apply=%region_5.0 | all-reduce | flops 1 | bytes 8 | tf_op jit(solution)/shard_map/psum | solution.py:32
  73.5 60.4 %all-reduce.3.cloned.1.call-done = (f32[8,128,128]{2,1,0:T(8,128)}, f32[8,128,128]{2,1,0:T(8,128)}) async-done(((f32[8,128,128]{2,1,0:T(8,128)}, f32[8,128,128]{2,1,0:T(8,128)}), (f32[8,128,128]{2,1,0:T(8,128)}, f32[8,128,128]{2,1,0:T(8,128)})) %all-reduce.3.cloned.1.call-update) | async-done | bytes 1048592 | tf_op jit(solution)/shard_map/psum | solution.py:45
  133.9 0.0 copy-start.2
  133.9 0.0 copy-start.4
  133.9 0.0 copy-start.13
  133.9 4.8 %bitcast_reduce_fusion = (f32[512,8]{0,1:T(8,128)S(1)}, f32[512,8]{0,1:T(8,128)S(1)}, f32[8,128,512]{2,1,0:T(8,128)S(1)}) fusion(f32[8,128]{1,0:T(8,128)S(1)} %bitcast.80, f32[512,8]{0,1:T(8,128)S(1)} %get-tuple-element.15, f32[512,8,128]{0,2,1:T(8,128)} %copy.57, f32[512,8]{0,1:T(8,128)S(1)} %broadcast_multiply_fusion.4, f32[512,8,128]{0,2,1:T(8,128)} %copy.55, ...), kind=kOutput, calls=%fused_computation.2 | convolution fusion | flops 140763136 | bytes 6928388 | tf_op jit(solution)/shard_map/nhi,hij->nhj/dot_general | solution.py:58
  138.7 0.0 copy-done.2
  138.7 0.0 copy-done.4
  138.7 0.0 copy-done.13
  138.7 1.7 %bitcast_reduce_fusion.1 = (f32[512,8]{0,1:T(8,128)S(1)}, f32[512,8]{0,1:T(8,128)S(1)}, f32[8,128,512]{2,1,0:T(8,128)S(1)}) fusion(f32[8,128]{1,0:T(8,128)S(1)} %bitcast.77, f32[512,8]{0,1:T(8,128)S(1)} %get-tuple-element.16, f32[512,8,128]{0,2,1:T(8,128)S(1)} %copy-done.4, f32[512,8]{0,1:T(8,128)S(1)} %broadcast_multiply_fusion.5, ...), kind=kOutput, calls=%fused_computation.9 | convolution fusion | flops 140763136 | bytes 6928388 | tf_op jit(solution)/shard_map/nhj,hij->nhi/dot_general | solution.py:57
  140.5 0.8 fusion.6
  141.3 0.0 copy-start.6
  141.3 0.0 copy-start.12
  141.3 1.3 fusion.21
  142.6 0.0 copy-start.9
  142.6 0.0 copy-done.6
  142.6 0.0 copy-done.12
  142.6 1.3 multiply_convert_fusion
  143.9 0.3 copy-done.9
  144.2 1.3 fusion.20
  145.5 0.0 copy-start.10
  145.5 0.8 fusion.2
  146.3 0.8 copy-done.10
  147.1 2.3 %add_convert_fusion = bf16[512,1024]{1,0:T(8,128)(2,1)} fusion(f32[512,1024]{1,0:T(8,128)S(1)} %fusion.20, f32[512,1024]{1,0:T(8,128)S(1)} %fusion.21, bf16[512,1024]{0,1:T(8,128)(2,1)S(1)} %bitcast.73, bf16[1024,1024]{1,0:T(8,128)(2,1)S(1)} %copy-done.10), kind=kOutput, calls=%fused_computation.14 | convolution fusion | flops 1075314688 | bytes 8388608 | tf_op jit(solution)/shard_map/dot_general | solution.py:63
  (8 shorter events, 0.0 us)
Async XLA Ops:
  6.5 10.4 %copy-start = (bf16[1024,1024]{1,0:T(8,128)(2,1)S(1)}, bf16[1024,1024]{1,0:T(8,128)(2,1)}, u32[]{:S(2)}) copy-start(bf16[1024,1024]{1,0:T(8,128)(2,1)} %param.14) | copy-start | bytes 6291460
  6.5 127.3 %all-reduce.3.cloned.1.call-start = ((), (), s32[]{:S(2)}) async-start(), calls=%async_computation | async-start | bytes 2097152 | tf_op jit(solution)/shard_map/psum | solution.py:45
  14.6 2.3 %copy-start.11 = (bf16[512,1024]{1,0:T(8,128)(2,1)S(1)}, bf16[512,1024]{1,0:T(8,128)(2,1)}, u32[]{:S(2)}) copy-start(bf16[512,1024]{1,0:T(8,128)(2,1)} %param.10) | copy-start | bytes 3145732
  31.7 2.2 %copy-start.3 = (f32[512,8,128]{0,2,1:T(8,128)S(1)}, f32[512,8,128]{0,2,1:T(8,128)}, u32[]{:S(2)}) copy-start(f32[512,8,128]{0,2,1:T(8,128)} %copy.55) | copy-start | bytes 6291460
  31.7 2.6 %copy-start.5 = (bf16[512,1024]{1,0:T(8,128)(2,1)S(1)}, bf16[512,1024]{1,0:T(8,128)(2,1)}, u32[]{:S(2)}) copy-start(bf16[512,1024]{1,0:T(8,128)(2,1)} %param.11) | copy-start | bytes 3145732
  33.9 1.7 %copy-start.1 = (f32[512,8,128]{0,2,1:T(8,128)S(1)}, f32[512,8,128]{0,2,1:T(8,128)}, u32[]{:S(2)}) copy-start(f32[512,8,128]{0,2,1:T(8,128)} %copy.57) | copy-start | bytes 6291460
  33.9 1.7 %copy-start.7 = (f32[1024]{0:T(1024)S(1)}, f32[1024]{0:T(1024)}, u32[]{:S(2)}) copy-start(f32[1024]{0:T(1024)} %param.16) | copy-start | bytes 12292
  33.9 1.7 %copy-start.8 = (f32[1024]{0:T(1024)S(1)}, f32[1024]{0:T(1024)}, u32[]{:S(2)}) copy-start(f32[1024]{0:T(1024)} %param.18) | copy-start | bytes 12292
  33.9 1.7 %copy-start.14 = (f32[1024]{0:T(1024)S(1)}, f32[1024]{0:T(1024)}, u32[]{:S(2)}) copy-start(f32[1024]{0:T(1024)} %param.17) | copy-start | bytes 12292
  33.9 1.7 %copy-start.15 = (f32[1024]{0:T(1024)S(1)}, f32[1024]{0:T(1024)}, u32[]{:S(2)}) copy-start(f32[1024]{0:T(1024)} %param.19) | copy-start | bytes 12292
  133.9 4.8 %copy-start.2 = (f32[512,8,128]{0,2,1:T(8,128)S(1)}, f32[512,8,128]{0,2,1:T(8,128)}, u32[]{:S(2)}) copy-start(f32[512,8,128]{0,2,1:T(8,128)} %copy.57) | copy-start | bytes 6291460
  133.9 4.8 %copy-start.4 = (f32[512,8,128]{0,2,1:T(8,128)S(1)}, f32[512,8,128]{0,2,1:T(8,128)}, u32[]{:S(2)}) copy-start(f32[512,8,128]{0,2,1:T(8,128)} %copy.55) | copy-start | bytes 6291460
  133.9 4.8 %copy-start.13 = (f32[8,128,128]{2,1,0:T(8,128)S(1)}, f32[8,128,128]{2,1,0:T(8,128)}, u32[]{:S(2)}) copy-start(f32[8,128,128]{2,1,0:T(8,128)} %get-tuple-element.10) | copy-start | bytes 1572868
  141.3 1.4 copy-start.6
  141.3 1.4 copy-start.12
  142.6 1.6 %copy-start.9 = (bf16[1024,1024]{1,0:T(8,128)(2,1)S(1)}, bf16[1024,1024]{1,0:T(8,128)(2,1)}, u32[]{:S(2)}) copy-start(bf16[1024,1024]{1,0:T(8,128)(2,1)} %param.13) | copy-start | bytes 6291460
  145.5 1.6 %copy-start.10 = (bf16[1024,1024]{1,0:T(8,128)(2,1)S(1)}, bf16[1024,1024]{1,0:T(8,128)(2,1)}, u32[]{:S(2)}) copy-start(bf16[1024,1024]{1,0:T(8,128)(2,1)} %param.15) | copy-start | bytes 6291460
Sparse Core Ops, SparseCore 0:
  37.7 96.1 all-reduce.2
where the time goes:
time: 157 us; the launch traced here: 156 us
  waiting for transfers between devices  60.4 us (38%)
  blocking collectives  35.9 us (23%)
  matrix products  24.6 us (16%)
  between operations  14.3 us (9%)
  local copies, waits for them, and re-layouts  12.5 us (8%)
  other arithmetic  8.47 us (5%)
    psum x1, waiting for transfers between devices, body(): kv_sum = lax.psum(kv_local, 'dx')  60.4 us
    psum x1, blocking collectives, body(): total = lax.psum(own_count, 'dx')  35.9 us
    reshape x2, local copies, waits for them, and re-layouts, head_norm(): grouped = raw.reshape(raw.shape[0], heads, -1)  5.92 us
    unnamed x34, local copies, waits for them, and re-layouts  4.87 us
    dot_general x1, matrix products, body(): jnp.einsum('nhi,hij->nhj', keys, dgram, preferred_element_type=jnp.float32)  4.81 us
    reduce_sum x2, other arithmetic, head_norm(): center = grouped - jnp.mean(grouped, axis=2, keepdims=True)  4.51 us
    dot_general x1, matrix products, body(): jnp.dot(points, w_query, preferred_element_type=jnp.float32)  4.15 us
    dot_general x1, matrix products, body(): jnp.dot(points, w_value, preferred_element_type=jnp.float32)  3.3 us
  transfers between devices with their start and end apart: 1, of which 1 were waited for; matrix products, arithmetic and copies ran while one was open for 0% of the time, Pallas kernels for 0%

commit v1 on v0

--- a/solution.py
+++ b/solution.py
@@ -42,7 +42,9 @@
     ).astype(jnp.bfloat16)
     kv_local = jnp.einsum("nhi,nhj->hij", keys, values, preferred_element_type=jnp.float32)
     cot = cotangent.reshape(rows, heads, -1)
-    kv_sum = lax.psum(kv_local, "dx")
+    kv_sum = kv_local
+    for hop in (1, 2, 4, 8):
+        kv_sum = kv_sum + lax.ppermute(kv_sum, "dx", [(dev, dev ^ hop) for dev in range(16)])
     query = jnp.dot(points, w_query, preferred_element_type=jnp.float32).astype(jnp.bfloat16)
     masked_query = (query * live.astype(jnp.bfloat16)).reshape(rows, heads, -1)
     qdy_local = jnp.einsum("nhi,nhj->hij", masked_query, cot, preferred_element_type=jnp.float32)

time: 157 us -> 180 us (1.15)
  waiting for transfers between devices: 60.4 us -> 82.5 us
    ppermute x0 -> x4, waiting for transfers between devices: none -> 48.5 us  [body(): lax.ppermute(kv_sum, 'dx', [(dev, dev ^ hop) for dev in range(16)])]
    psum x1, waiting for transfers between devices: 60.4 us -> 33.9 us  [body(): qdy_sum = lax.psum(qdy_local, 'dx')]
    unnamed x34 -> x30, local copies, waits for them, and re-layouts: 4.87 us -> 4.33 us
  transfers between devices with their start and end apart: 1 -> 5, of which waited for: 1 -> 4; matrix products, arithmetic and copies ran while one was open for 0% -> 17% of each run, Pallas kernels for 0% -> 0%
where the time goes in v1:
time: 180 us; the launch traced here: 179 us
  waiting for transfers between devices  82.5 us (46%)
  blocking collectives  35.9 us (20%)
  matrix products  24.5 us (14%)
  between operations  14.5 us (8%)
  local copies, waits for them, and re-layouts  11.9 us (7%)
  other arithmetic  8.67 us (5%)
    ppermute x4, waiting for transfers between devices, body(): lax.ppermute(kv_sum, 'dx', [(dev, dev ^ hop) for dev in range(16)])  48.5 us
    psum x1, blocking collectives, body(): total = lax.psum(own_count, 'dx')  35.9 us
    psum x1, waiting for transfers between devices, body(): qdy_sum = lax.psum(qdy_local, 'dx')  33.9 us
    reshape x2, local copies, waits for them, and re-layouts, head_norm(): grouped = raw.reshape(raw.shape[0], heads, -1)  5.92 us
    dot_general x1, matrix products, body(): jnp.einsum('nhi,hij->nhj', keys, dgram, preferred_element_type=jnp.float32)  4.71 us
    reduce_sum x2, other arithmetic, head_norm(): center = grouped - jnp.mean(grouped, axis=2, keepdims=True)  4.53 us
    unnamed x30, local copies, waits for them, and re-layouts  4.33 us
    dot_general x1, matrix products, body(): jnp.dot(points, w_query, preferred_element_type=jnp.float32)  4.15 us
  transfers between devices with their start and end apart: 5, of which 4 were waited for; matrix products, arithmetic and copies ran while one was open for 17% of the time, Pallas kernels for 0%

profile of v1, /device:TPU:0, one launch (start us, length us, event | category | flops | bytes accessed | tf_op | source)
XLA Modules:
  0.0 179.4 jit_solution(9983139068857051653)
XLA Ops:
  6.5 0.0 copy-start
  6.5 0.0 all-reduce.2.cloned.1.call-start
  7.4 4.1 %fusion.8 = bf16[512,1024]{1,0:T(8,128)(2,1)} fusion(bf16[512,1024]{1,0:T(8,128)(2,1)} %param.10, bf16[1024,1024]{1,0:T(8,128)(2,1)} %param.13, bf16[512]{0:T(512)(128)(2,1)S(1)} %fusion.16), kind=kOutput, calls=%fused_computation.25 | convolution fusion | flops 1074790400 | bytes 4195328 | tf_op jit(solution)/shard_map/dot_general | solution.py:48
  11.5 1.5 copy.71
  13.0 2.5 %fusion.9 = f32[8,128,128]{2,1,0:T(8,128)} fusion(bf16[512,8,128]{0,2,1:T(8,128)(2,1)S(1)} %bitcast.73, bf16[512,1024]{1,0:T(8,128)(2,1)} %param.11), kind=kOutput, calls=%fused_computation.26 | convolution fusion | flops 134217728 | bytes 2621440 | tf_op jit(solution)/shard_map/nhi,nhj->hij/dot_general | solution.py:50
  15.5 0.0 all-reduce.2.cloned.1.call-update
  15.5 3.2 %convolution_bitcast_fusion = f32[64,8,8,128]{3,1,2,0:T(8,128)S(1)} fusion(bf16[512,1024]{1,0:T(8,128)(2,1)} %param.10, bf16[1024,1024]{1,0:T(8,128)(2,1)} %param.15), kind=kOutput, calls=%fused_computation.22 | convolution fusion | flops 1073741824 | bytes 5242880 | tf_op jit(solution)/shard_map/dot_general | solution.py:35
  18.7 1.8 copy.74
  20.4 3.0 %copy.59 = f32[512,8,128]{0,2,1:T(8,128)} copy(f32[512,8,128]{2,1,0:T(8,128)} %bitcast.71) | data formatting | bytes 4194304 | tf_op jit(solution)/shard_map/reshape | solution.py:11
  23.4 0.0 copy-start.10
  23.4 2.3 %reduce_sum.74 = f32[512,8]{1,0:T(8,128)S(1)} reduce(f32[512,8,128]{2,1,0:T(8,128)} %bitcast.72, f32[]{:T(128)} %constant.11.clone.1), dimensions={2}, to_apply=%region_2.0 | reduce | flops 520192 | bytes 2113540 | tf_op jit(solution)/shard_map/reduce_sum | solution.py:12
  25.7 0.0 copy-done
  25.7 0.0 copy-done.10
  25.8 1.2 convolution_bitcast_fusion.1
  27.0 1.8 copy.73
  28.8 2.9 %copy.57 = f32[512,8,128]{0,2,1:T(8,128)} copy(f32[512,8,128]{2,1,0:T(8,128)} %bitcast.69) | data formatting | bytes 4194304 | tf_op jit(solution)/shard_map/reshape | solution.py:11
  31.7 2.2 %reduce_sum.72 = f32[512,8]{1,0:T(8,128)S(1)} reduce(f32[512,8,128]{2,1,0:T(8,128)} %bitcast.70, f32[]{:T(128)} %constant.11.clone.1), dimensions={2}, to_apply=%region_0.0 | reduce | flops 520192 | bytes 2113540 | tf_op jit(solution)/shard_map/reduce_sum | solution.py:12
  34.0 0.1 copy.58
  34.1 0.1 copy.56
  34.2 0.0 copy-start.1
  34.2 0.0 copy-start.3
  34.2 0.0 copy-start.6
  34.2 0.0 copy-start.7
  34.2 0.0 copy-start.12
  34.2 0.0 copy-start.13
  34.3 2.1 %multiply_reduce_fusion = f32[512,8]{0,1:T(8,128)S(1)} fusion(f32[512,8,128]{0,2,1:T(8,128)} %copy.59, f32[512,8]{0,1:T(8,128)S(1)} %broadcast_multiply_fusion.4), kind=kLoop, calls=%fused_computation.17 | loop fusion | flops 1568768 | bytes 2129920 | tf_op jit(solution)/shard_map/reduce_sum | solution.py:13
  36.3 0.1 copy-done.1
  36.4 0.3 multiply_reduce_fusion.1
  36.8 0.3 copy-done.3
  37.1 0.0 copy-done.6
  37.1 0.0 copy-done.7
  37.1 0.0 copy-done.12
  37.1 0.0 copy-done.13
  37.1 1.1 fusion.18
  38.2 0.5 collective-permute-start
  38.8 35.9 %psum.14 = f32[]{:T(128)} all-reduce(f32[]{:T(128)S(6)} %convert_element_type.64), channel_id=1, replica_groups=mesh['group'=2,'dx'=16] {'dx'}, use_global_device_ids=true, to_apply=%region_4.0 | all-reduce | flops 1 | bytes 8 | tf_op jit(solution)/shard_map/psum | solution.py:32
  74.6 33.9 %all-reduce.2.cloned.1.call-done = f32[8,128,128]{2,1,0:T(8,128)} async-done(((f32[8,128,128]{2,1,0:T(8,128)}), f32[8,128,128]{2,1,0:T(8,128)}) %all-reduce.2.cloned.1.call-update) | async-done | bytes 524304 | tf_op jit(solution)/shard_map/psum | solution.py:51
  108.5 4.7 %bitcast_reduce_fusion = (f32[512,8]{0,1:T(8,128)S(1)}, f32[512,8]{0,1:T(8,128)S(1)}, f32[8,128,512]{2,1,0:T(8,128)S(1)}) fusion(f32[8,128]{1,0:T(8,128)S(1)} %bitcast.77, f32[512,8]{0,1:T(8,128)S(1)} %get-tuple-element.11, f32[512,8,128]{0,2,1:T(8,128)} %copy.59, f32[512,8]{0,1:T(8,128)S(1)} %broadcast_multiply_fusion.4, f32[512,8,128]{0,2,1:T(8,128)} %copy.57, ...), kind=kOutput, calls=%fused_computation.2 | convolution fusion | flops 140763136 | bytes 6928388 | tf_op jit(solution)/shard_map/nhi,hij->nhj/dot_general | solution.py:60
  113.3 0.0 copy-done.2
  113.3 0.0 copy-done.4
  113.3 0.0 copy-done.11
  113.3 1.6 bitcast_reduce_fusion.1
  114.9 0.0 collective-permute-done
  114.9 0.1 add.66
  115.0 0.7 collective-permute-start.1
  115.6 13.7 %collective-permute-done.1 = f32[8,128,128]{2,1,0:T(8,128)S(1)} collective-permute-done((f32[8,128,128]{2,1,0:T(8,128)S(1)}, f32[8,128,128]{2,1,0:T(8,128)S(1)}, u32[]{:S(2)}, u32[]{:S(2)}) %collective-permute-start.1) | collective-permute-done | bytes 524320 | tf_op jit(solution)/shard_map/ppermute | solution.py:47
  129.3 0.1 add.67
  129.4 0.3 collective-permute-start.2
  129.7 0.8 fusion.2
  130.5 12.5 %collective-permute-done.2 = f32[8,128,128]{2,1,0:T(8,128)S(1)} collective-permute-done((f32[8,128,128]{2,1,0:T(8,128)S(1)}, f32[8,128,128]{2,1,0:T(8,128)S(1)}, u32[]{:S(2)}, u32[]{:S(2)}) %collective-permute-start.2) | collective-permute-done | bytes 524320 | tf_op jit(solution)/shard_map/ppermute | solution.py:47
  143.0 0.1 add.68
  143.0 0.1 collective-permute-start.3
  143.1 0.8 fusion.6
  143.9 0.0 copy-start.5
  143.9 1.3 fusion.21
  145.2 0.0 copy-start.8
  145.2 22.4 %collective-permute-done.3 = f32[8,128,128]{2,1,0:T(8,128)S(1)} collective-permute-done((f32[8,128,128]{2,1,0:T(8,128)S(1)}, f32[8,128,128]{2,1,0:T(8,128)S(1)}, u32[]{:S(2)}, u32[]{:S(2)}) %collective-permute-start.3) | collective-permute-done | bytes 524320 | tf_op jit(solution)/shard_map/ppermute | solution.py:47
  167.6 0.0 copy-done.5
  167.6 1.1 multiply_convert_fusion
  168.7 0.0 copy-done.8
  168.7 0.0 copy-start.9
  168.7 1.3 fusion.20
  170.0 0.3 copy-done.9
  170.3 2.3 %add_convert_fusion = bf16[512,1024]{1,0:T(8,128)(2,1)} fusion(f32[512,1024]{1,0:T(8,128)S(1)} %fusion.20, f32[512,1024]{1,0:T(8,128)S(1)} %fusion.21, bf16[512,1024]{0,1:T(8,128)(2,1)S(1)} %bitcast.74, bf16[1024,1024]{1,0:T(8,128)(2,1)S(1)} %copy-done.9), kind=kOutput, calls=%fused_computation.14 | convolution fusion | flops 1075314688 | bytes 8388608 | tf_op jit(solution)/shard_map/dot_general | solution.py:65
  (12 shorter events, 0.1 us)
Async XLA Ops:
  6.5 19.2 %copy-start = (bf16[1024,1024]{1,0:T(8,128)(2,1)S(1)}, bf16[1024,1024]{1,0:T(8,128)(2,1)}, u32[]{:S(2)}) copy-start(bf16[1024,1024]{1,0:T(8,128)(2,1)} %param.14) | copy-start | bytes 6291460
  6.5 102.0 %all-reduce.2.cloned.1.call-start = ((), (), s32[]{:S(2)}) async-start(), calls=%async_computation | async-start | bytes 1048576 | tf_op jit(solution)/shard_map/psum | solution.py:51
  23.4 2.3 %copy-start.10 = (bf16[512,1024]{1,0:T(8,128)(2,1)S(1)}, bf16[512,1024]{1,0:T(8,128)(2,1)}, u32[]{:S(2)}) copy-start(bf16[512,1024]{1,0:T(8,128)(2,1)} %param.10) | copy-start | bytes 3145732
  34.2 2.3 %copy-start.1 = (f32[512,8,128]{0,2,1:T(8,128)S(1)}, f32[512,8,128]{0,2,1:T(8,128)}, u32[]{:S(2)}) copy-start(f32[512,8,128]{0,2,1:T(8,128)} %copy.57) | copy-start | bytes 6291460
  34.2 2.9 %copy-start.3 = (f32[512,8,128]{0,2,1:T(8,128)S(1)}, f32[512,8,128]{0,2,1:T(8,128)}, u32[]{:S(2)}) copy-start(f32[512,8,128]{0,2,1:T(8,128)} %copy.59) | copy-start | bytes 6291460
  34.2 2.9 %copy-start.6 = (f32[1024]{0:T(1024)S(1)}, f32[1024]{0:T(1024)}, u32[]{:S(2)}) copy-start(f32[1024]{0:T(1024)} %param.18) | copy-start | bytes 12292
  34.2 2.9 %copy-start.7 = (f32[1024]{0:T(1024)S(1)}, f32[1024]{0:T(1024)}, u32[]{:S(2)}) copy-start(f32[1024]{0:T(1024)} %param.16) | copy-start | bytes 12292
  34.2 2.8 %copy-start.12 = (f32[1024]{0:T(1024)S(1)}, f32[1024]{0:T(1024)}, u32[]{:S(2)}) copy-start(f32[1024]{0:T(1024)} %param.17) | copy-start | bytes 12292
  34.2 2.8 %copy-start.13 = (f32[1024]{0:T(1024)S(1)}, f32[1024]{0:T(1024)}, u32[]{:S(2)}) copy-start(f32[1024]{0:T(1024)} %param.19) | copy-start | bytes 12292
  38.2 76.7 %collective-permute-start = (f32[8,128,128]{2,1,0:T(8,128)S(1)}, f32[8,128,128]{2,1,0:T(8,128)S(1)}, u32[]{:S(2)}, u32[]{:S(2)}) collective-permute-start(f32[8,128,128]{2,1,0:T(8,128)S(1)} %fusion.18), channel_id=1, source_target_pairs={{0,1},{1,0},{2,3},{3,2},{4,5},{5,4},{6,7},{7,6},{8,9},{9,8},{10,11... | collective-permute-start | bytes 1572872 | tf_op jit(solution)/shard_map/ppermute | solution.py:47
  108.5 4.7 %copy-start.2 = (f32[512,8,128]{0,2,1:T(8,128)S(1)}, f32[512,8,128]{0,2,1:T(8,128)}, u32[]{:S(2)}) copy-start(f32[512,8,128]{0,2,1:T(8,128)} %copy.57) | copy-start | bytes 6291460
  108.5 4.7 %copy-start.4 = (f32[512,8,128]{0,2,1:T(8,128)S(1)}, f32[512,8,128]{0,2,1:T(8,128)}, u32[]{:S(2)}) copy-start(f32[512,8,128]{0,2,1:T(8,128)} %copy.59) | copy-start | bytes 6291460
  108.5 4.7 %copy-start.11 = (f32[8,128,128]{2,1,0:T(8,128)S(1)}, f32[8,128,128]{2,1,0:T(8,128)}, u32[]{:S(2)}) copy-start(f32[8,128,128]{2,1,0:T(8,128)} %all-reduce.2.cloned.1.call-done) | copy-start | bytes 1572868
  115.0 14.4 %collective-permute-start.1 = (f32[8,128,128]{2,1,0:T(8,128)S(1)}, f32[8,128,128]{2,1,0:T(8,128)S(1)}, u32[]{:S(2)}, u32[]{:S(2)}) collective-permute-start(f32[8,128,128]{2,1,0:T(8,128)S(1)} %add.66), channel_id=1, source_target_pairs={{0,2},{1,3},{2,0},{3,1},{4,6},{5,7},{6,4},{7,5},{8,10},{9,11},{10,... | collective-permute-start | bytes 1572872 | tf_op jit(solution)/shard_map/ppermute | solution.py:47
  129.4 13.6 %collective-permute-start.2 = (f32[8,128,128]{2,1,0:T(8,128)S(1)}, f32[8,128,128]{2,1,0:T(8,128)S(1)}, u32[]{:S(2)}, u32[]{:S(2)}) collective-permute-start(f32[8,128,128]{2,1,0:T(8,128)S(1)} %add.67), channel_id=1, source_target_pairs={{0,4},{1,5},{2,6},{3,7},{4,0},{5,1},{6,2},{7,3},{8,12},{9,13},{10,... | collective-permute-start | bytes 1572872 | tf_op jit(solution)/shard_map/ppermute | solution.py:47
  143.0 24.6 %collective-permute-start.3 = (f32[8,128,128]{2,1,0:T(8,128)S(1)}, f32[8,128,128]{2,1,0:T(8,128)S(1)}, u32[]{:S(2)}, u32[]{:S(2)}) collective-permute-start(f32[8,128,128]{2,1,0:T(8,128)S(1)} %add.68), channel_id=1, source_target_pairs={{0,8},{1,9},{2,10},{3,11},{4,12},{5,13},{6,14},{7,15},{8,0},{9,1},... | collective-permute-start | bytes 1572872 | tf_op jit(solution)/shard_map/ppermute | solution.py:47
  143.9 23.7 %copy-start.5 = (bf16[512,1024]{1,0:T(8,128)(2,1)S(1)}, bf16[512,1024]{1,0:T(8,128)(2,1)}, u32[]{:S(2)}) copy-start(bf16[512,1024]{1,0:T(8,128)(2,1)} %param.11) | copy-start | bytes 3145732
  145.2 23.5 %copy-start.8 = (bf16[1024,1024]{1,0:T(8,128)(2,1)S(1)}, bf16[1024,1024]{1,0:T(8,128)(2,1)}, u32[]{:S(2)}) copy-start(bf16[1024,1024]{1,0:T(8,128)(2,1)} %param.13) | copy-start | bytes 6291460
  168.7 1.6 copy-start.9
Sparse Core Ops, SparseCore 0:
  15.6 92.8 all-reduce.1
